TPU v7x, 32 devices: a whole 2x2x4 slice. The times are simulated.
32 devices in a mesh: mesh: 8 (over z, y), comb: 4 (over x, core).
Axes of the slice: x: 2, y: 2, z: 4, core: 2. Of those that a mesh axis runs over, the one named last changes fastest.
Arguments:
- coeffs: bfloat16 [1024, 512], P('comb'), may hold values from -3 to 3
- basis: bfloat16 [3, 4096, 512], P(None, 'mesh', 'comb'), may hold values from -0.25 to 0.25
- connect: int32 [32, 4, 128], P('mesh'), may hold values from 0 to 767
- stiffness: float32 [32, 128], P('mesh'), may hold values from 0.3 to 3
- send_lists: int32 [8, 2, 128], P('mesh'), may hold values from 0 to 511, as said below
- elem_count: int32 [8], P('mesh'), may hold values from 128 to 512, as said below
Outputs:
- modal_force: float32 [1024, 512], P('comb', 'mesh')
Inputs may be any that keep to these rules, and one draw needn't show every extreme that they name: `connect`: slots below 512 are the partition's own nodes, then 128 slots lent by the lower neighbour and 128 lent by the upper one; entries of element slots that are not live are arbitrary valid slots. `send_lists`: the 128 entries of each row are distinct local node numbers. `elem_count`: some partition is full and some holds a quarter of 512.
All inputs are finite; a program needn't handle non-finite values.
Results may differ from a plain program's by a relative error of at most 0.00071.
Values may be sent and summed in bfloat16 or wider, within the bound.
A program may use at most 64 MiB of HBM per device.

v0:
```python
import jax
import jax.numpy as jnp
from jax import lax
from jax.sharding import PartitionSpec as P

stiff_cubic = 0.3
twist_ratio = 0.5


def with_halo(shard, sides, width):
    for axis, dim in sides:
        size, length = (lax.axis_size(axis), shard.shape[dim])
        up = [(i, (i + 1) % size) for i in range(size - 1)]
        down = [(j, i) for i, j in up]
        last = lax.slice_in_dim(shard, length - width, length, axis=dim)
        leading = lax.slice_in_dim(shard, 0, width, axis=dim)
        before = lax.ppermute(last, axis, up)
        after = lax.ppermute(leading, axis, down)
        shard = jnp.concatenate([before, shard, after], axis=dim)
    return shard


def spring_pull(start_node, end_node, stiff_now):
    stretch = end_node - start_node
    factor = stiff_now * (1.0 + stiff_cubic * jnp.sum(stretch * stretch, axis=1, keepdims=True))
    return factor * stretch


def element_forces(corners, stiff_now):
    points = [corners[0], corners[1], corners[2], corners[3]]
    totals = [jnp.zeros_like(points[0]) for unused in range(4)]
    edge_pairs = [(0, 1), (1, 2), (2, 3), (3, 0), (0, 2), (1, 3)]
    for lower_end, upper_end in edge_pairs:
        tension = spring_pull(points[lower_end], points[upper_end], stiff_now)
        totals[upper_end] = totals[upper_end] + tension
        totals[lower_end] = totals[lower_end] - tension
    twist = twist_ratio * stiff_now * (points[0] - points[1] + points[2] - points[3])
    totals[0] = totals[0] + twist
    totals[1] = totals[1] - twist
    totals[2] = totals[2] + twist
    totals[3] = totals[3] - twist
    return jnp.stack(totals, axis=0)


def body(coeffs, basis, connect, stiffness, send_lists, elem_count):
    node_rows = basis.shape[1]
    ghost_rows = send_lists.shape[2]
    comb_rows = coeffs.shape[0]
    chosen = send_lists[0]
    whole_basis = lax.all_gather(basis, "comb", axis=2, tiled=True)
    displaced = jnp.einsum(
        "cm,dnm->ndc", coeffs, whole_basis, preferred_element_type=jnp.float32
    ).astype(jnp.bfloat16)
    rim_disp = displaced[chosen]
    disp_halo = with_halo(rim_disp, (("mesh", 0),), 1)
    displaced = jnp.concatenate([displaced, disp_halo[0], disp_halo[3]], axis=0)
    slot_width = displaced.shape[0]
    lane_ids = jnp.arange(128, dtype=jnp.int32)
    live_count = elem_count[0]

    def add_block(block_id, forces):
        slot_ids = lax.dynamic_index_in_dim(connect, block_id, 0, keepdims=False).reshape(-1)
        stiff_now = lax.dynamic_index_in_dim(stiffness, block_id, 0, keepdims=False)
        stiff_now = jnp.where(block_id * 128 + lane_ids < live_count, stiff_now, jnp.float32(0.0))
        corners = (
            jnp.take(displaced, slot_ids, axis=0).astype(jnp.float32).reshape(4, 128, 3, comb_rows)
        )
        pushed = element_forces(corners, stiff_now[:, None, None])
        return forces.at[slot_ids].add(pushed.reshape(512, 3, comb_rows))

    forces = lax.fori_loop(
        0, (live_count + 127) // 128, add_block, jnp.zeros((slot_width, 3, comb_rows), jnp.float32)
    )
    nodal_force = forces.astype(jnp.bfloat16)
    modal = jnp.einsum(
        "ndc,dnm->cm", nodal_force[:node_rows], whole_basis, preferred_element_type=jnp.float32
    )
    borrowed = nodal_force[node_rows:].reshape(2, ghost_rows, 3, comb_rows)
    returned = with_halo(borrowed, (("mesh", 0),), 1)
    back_rows = jnp.stack([returned[0], returned[3]], axis=0)
    modal = modal + jnp.einsum(
        "kgdc,dkgm->cm", back_rows, whole_basis[:, chosen, :], preferred_element_type=jnp.float32
    )
    out_scale = (whole_basis.shape[2] / (3.0 * node_rows * lax.axis_size("mesh"))) ** 0.5
    return lax.psum_scatter(modal * out_scale, "mesh", scatter_dimension=1, tiled=True)


def solution(mesh):
    in_specs = (
        P("comb", None),
        P(None, "mesh", "comb"),
        P("mesh", None, None),
        P("mesh", None),
        P("mesh", None, None),
        P("mesh"),
    )
    out_specs = P("comb", "mesh")
    return jax.shard_map(body, mesh=mesh, in_specs=in_specs, out_specs=out_specs, check_vma=False)
```

profile of v0, /device:TPU:0, one launch (start us, length us, event | category | flops | bytes accessed | tf_op | source)
XLA Modules:
  0.0 392.3 jit_solution(10388399615611316061)
XLA Ops:
  8.0 23.5 %all-gather.2.cloned.1.call-done = bf16[3,512,512]{2,1,0:T(8,128)(2,1)} async-done(((bf16[3,512,128]{2,1,0:T(8,128)(2,1)}), bf16[3,512,512]{2,1,0:T(8,128)(2,1)}) %all-gather.2.cloned.1.call-update) | async-done | bytes 1572880 | tf_op jit(solution)/shard_map/all_gather | solution.py:50
  31.5 2.0 fusion.2
  33.5 1.7 copy.12
  35.2 2.4 gather_fusion.1
  37.8 3.4 collective-permute-start
  43.2 2.7 copy.18
  45.9 3.1 gather_fusion.2
  49.0 1.5 copy.19
  50.6 2.2 copy.15
  52.8 2.1 broadcast_in_dim.16
  54.9 252.3 %while.11 = (s32[]{:T(128)}, f32[768,3,256]{2,1,0:T(4,128)}, s32[]{:T(128)}, s32[4,4,128]{2,1,0:T(4,128)}, s32[]{:T(128)}, /*index=5*/f32[4,128]{1,0:T(4,128)}, ...) while((s32[]{:T(128)}, f32[768,3,256]{2,1,0:T(4,128)}, ...), condition=%wide.region_8.9_spmd.clone, body=%wide.region_0.8_spmd.clone.sunk | while | flops 7968774 | bytes 22435500 | solution.py:71
  55.6 3.2 gather_fusion
  58.8 1.8 select_convert_fusion.2
  60.6 2.2 multiply_reduce_fusion.7
  66.0 51.9 %scatter_fusion = f32[768,3,256]{2,1,0:T(4,128)} fusion(f32[768,3,256]{2,1,0:T(4,128)} %get-tuple-element.217, s32[512]{0:T(512)S(1)} %bitcast.72, f32[512,3,256]{2,1,0:T(4,128)S(1)} %bitcast.69), kind=kCustom, calls=%fused_computation.3.clone.clone.1 | custom fusion | flops 393216 | bytes 4720640 | tf_op jit(solution)/shard_map/while/body/scatter-add | solution.py:69
  118.6 3.2 gather_fusion
  121.8 1.8 select_convert_fusion.2
  123.6 2.2 multiply_reduce_fusion.7
  129.0 52.1 %scatter_fusion = f32[768,3,256]{2,1,0:T(4,128)} fusion(f32[768,3,256]{2,1,0:T(4,128)} %get-tuple-element.217, s32[512]{0:T(512)S(1)} %bitcast.72, f32[512,3,256]{2,1,0:T(4,128)S(1)} %bitcast.69), kind=kCustom, calls=%fused_computation.3.clone.clone.1 | custom fusion | flops 393216 | bytes 4720640 | tf_op jit(solution)/shard_map/while/body/scatter-add | solution.py:69
  181.8 3.2 gather_fusion
  185.0 1.8 select_convert_fusion.2
  186.8 2.2 multiply_reduce_fusion.7
  192.2 51.9 %scatter_fusion = f32[768,3,256]{2,1,0:T(4,128)} fusion(f32[768,3,256]{2,1,0:T(4,128)} %get-tuple-element.217, s32[512]{0:T(512)S(1)} %bitcast.72, f32[512,3,256]{2,1,0:T(4,128)S(1)} %bitcast.69), kind=kCustom, calls=%fused_computation.3.clone.clone.1 | custom fusion | flops 393216 | bytes 4720640 | tf_op jit(solution)/shard_map/while/body/scatter-add | solution.py:69
  244.8 3.2 gather_fusion
  248.0 1.8 select_convert_fusion.2
  249.8 2.2 multiply_reduce_fusion.7
  255.2 52.0 %scatter_fusion = f32[768,3,256]{2,1,0:T(4,128)} fusion(f32[768,3,256]{2,1,0:T(4,128)} %get-tuple-element.217, s32[512]{0:T(512)S(1)} %bitcast.72, f32[512,3,256]{2,1,0:T(4,128)S(1)} %bitcast.69), kind=kCustom, calls=%fused_computation.3.clone.clone.1 | custom fusion | flops 393216 | bytes 4720640 | tf_op jit(solution)/shard_map/while/body/scatter-add | solution.py:69
  307.2 2.4 copy.30
  309.6 1.4 collective-permute-start.2
  313.1 2.5 collective-permute-done.2
  315.6 4.1 %collective-permute-done.3 = bf16[1,128,3,256]{3,1,2,0:T(8,128)(2,1)S(1)} collective-permute-done((bf16[1,128,3,256]{3,1,2,0:T(8,128)(2,1)S(1)}, bf16[1,128,3,256]{3,1,2,0:T(8,128)(2,1)S(1)}, u32[]{:S(2)}, u32[]{:S(2)}) %collective-permute-start.3) | collective-permute-done | bytes 196640 | tf_op jit(solution)/shard_map/ppermute | solution.py:18
  320.9 64.6 %reduce-scatter.2.cloned.1.call-done = f32[256,64]{0,1:T(8,128)} async-done(((f32[256,512]{0,1:T(8,128)}), f32[256,64]{0,1:T(8,128)}) %reduce-scatter.2.cloned.1.call-update) | async-done | bytes 65552 | tf_op jit(solution)/shard_map/reduce_scatter | solution.py:85
  (57 shorter events, 21.8 us)
Async XLA Ops:
  6.5 24.9 %copy-start = (bf16[256,512]{1,0:T(8,128)(2,1)S(1)}, bf16[256,512]{1,0:T(8,128)(2,1)}, u32[]{:S(2)}) copy-start(bf16[256,512]{1,0:T(8,128)(2,1)} %param.8) | copy-start | bytes 786436
  6.5 24.9 %all-gather.2.cloned.1.call-start = ((), (), s32[]{:S(2)}) async-start(), calls=%async_computation.1 | async-start | bytes 1966080 | tf_op jit(solution)/shard_map/all_gather | solution.py:50
  7.3 378.2 %reduce-scatter.2.cloned.1.call-start = ((), (), s32[]{:S(2)}) async-start(), calls=%async_computation.2 | async-start | bytes 589824 | tf_op jit(solution)/shard_map/reduce_scatter | solution.py:85
  33.5 9.7 %copy-start.1 = (bf16[3,512,512]{2,1,0:T(8,128)(2,1)S(1)}, bf16[3,512,512]{2,1,0:T(8,128)(2,1)}, u32[]{:S(2)}) copy-start(bf16[3,512,512]{2,1,0:T(8,128)(2,1)} %all-gather.2.cloned.1.call-done) | copy-start | bytes 4718596
  37.8 12.8 %collective-permute-start = (bf16[1,128,3,256]{3,1,2,0:T(8,128)(2,1)S(1)}, bf16[1,128,3,256]{3,1,2,0:T(8,128)(2,1)S(1)}, u32[]{:S(2)}, u32[]{:S(2)}) collective-permute-start(bf16[1,128,3,256]{3,1,2,0:T(8,128)(2,1)S(1)} %bitcast.75), channel_id=1, source_target_pairs={{0,4},{4,8},{8,12},{12,16},{16,20},{20,24},{24,28},{1,5},{5,9},{9,... | collective-permute-start | bytes 589832 | tf_op jit(solution)/shard_map/ppermute | solution.py:17
  41.2 9.3 %collective-permute-start.1 = (bf16[1,128,3,256]{3,1,2,0:T(8,128)(2,1)S(1)}, bf16[1,128,3,256]{3,1,2,0:T(8,128)(2,1)S(1)}, u32[]{:S(2)}, u32[]{:S(2)}) collective-permute-start(bf16[1,128,3,256]{3,1,2,0:T(8,128)(2,1)S(1)} %bitcast.77), channel_id=1, source_target_pairs={{4,0},{8,4},{12,8},{16,12},{20,16},{24,20},{28,24},{5,1},{9,5},{13... | collective-permute-start | bytes 589832 | tf_op jit(solution)/shard_map/ppermute | solution.py:18
  307.2 5.1 %copy-start.2 = (bf16[3,512,512]{2,1,0:T(8,128)(2,1)S(1)}, bf16[3,512,512]{2,1,0:T(8,128)(2,1)}, u32[]{:S(2)}) copy-start(bf16[3,512,512]{2,1,0:T(8,128)(2,1)} %all-gather.2.cloned.1.call-done) | copy-start | bytes 4718596
  309.5 10.2 %copy-start.3 = (bf16[2,128,3,512]{1,3,0,2:T(8,128)(2,1)S(1)}, bf16[2,128,3,512]{1,3,0,2:T(8,128)(2,1)}, u32[]{:S(2)}) copy-start(bf16[2,128,3,512]{1,3,0,2:T(8,128)(2,1)} %copy.19) | copy-start | bytes 2359300
  309.6 6.0 %collective-permute-start.2 = (bf16[1,128,3,256]{3,1,2,0:T(8,128)(2,1)S(1)}, bf16[1,128,3,256]{3,1,2,0:T(8,128)(2,1)S(1)}, u32[]{:S(2)}, u32[]{:S(2)}) collective-permute-start(bf16[1,128,3,256]{3,1,2,0:T(8,128)(2,1)S(1)} %get-tuple-element.115), channel_id=1, source_target_pairs={{0,4},{4,8},{8,12},{12,16},{16,20},{20,24},{24,28},{1,5},{5,9},{9,... | collective-permute-start | bytes 589832 | tf_op jit(solution)/shard_map/ppermute | solution.py:17
  311.0 8.7 %collective-permute-start.3 = (bf16[1,128,3,256]{3,1,2,0:T(8,128)(2,1)S(1)}, bf16[1,128,3,256]{3,1,2,0:T(8,128)(2,1)S(1)}, u32[]{:S(2)}, u32[]{:S(2)}) collective-permute-start(bf16[1,128,3,256]{3,1,2,0:T(8,128)(2,1)S(1)} %get-tuple-element.116), channel_id=1, source_target_pairs={{4,0},{8,4},{12,8},{16,12},{20,16},{24,20},{28,24},{5,1},{9,5},{13... | collective-permute-start | bytes 589832 | tf_op jit(solution)/shard_map/ppermute | solution.py:18
Sparse Core Ops, SparseCore 0:
  8.9 22.5 all-gather.1
  321.0 64.4 reduce-scatter.1
where the time goes:
time: 400 us; the launch traced here: 392 us
  other arithmetic  240 us (60%)
  waiting for transfers between devices  95.4 us (24%)
  local copies, waits for them, and re-layouts  31.2 us (8%)
  between operations  14.2 us (4%)
  starting transfers between devices  7.46 us (2%)
    scatter-add x4, other arithmetic, add_block(): return forces.at[slot_ids].add(pushed.reshape(512, 3, comb_rows))  208 us
    reduce_scatter x1, waiting for transfers between devices, body(): lax.psum_scatter(modal * out_scale, 'mesh', scatter_dimension=1, tiled=True)  64.6 us
    all_gather x1, waiting for transfers between devices, body(): whole_basis = lax.all_gather(basis, 'comb', axis=2, tiled=True)  23.5 us
    gather x4, local copies, waits for them, and re-layouts, add_block(): jnp.take(displaced, slot_ids, axis=0).astype(jnp.float32)  12.9 us
    reduce_sum x4, other arithmetic, spring_pull(): jnp.sum(stretch * stretch, axis=1, keepdims=True)  8.76 us
  transfers between devices with their start and end apart: 6, of which 4 were waited for; matrix products, arithmetic and copies ran while one was open for 2% of the time, Pallas kernels for 0%

commit v1 on v0

--- a/solution.py
+++ b/solution.py
@@ -1,10 +1,15 @@
+import functools
+
 import jax
 import jax.numpy as jnp
 from jax import lax
+from jax.experimental import pallas as pl
+from jax.experimental.pallas import tpu as pltpu
 from jax.sharding import PartitionSpec as P
 
 stiff_cubic = 0.3
 twist_ratio = 0.5
+MESH = pl.DeviceIdType.MESH
 
 
 def with_halo(shard, sides, width):
@@ -85,6 +90,310 @@
     return lax.psum_scatter(modal * out_scale, "mesh", scatter_dimension=1, tiled=True)
 
 
+def fused_kernel(n_mesh, coeffs_ref, basis_ref, connect_ref, stiff_ref, send_ref, count_ref, out_ref,
+                 coef_s, wide, inc, lent_onehot, lent_own, lent_far, disp_v, force_s, modal_acc,
+                 part_out, part_in,
+                 s_mate, r_mate, s_far, r_far, s_fwd, r_fwd, s_lent, r_lent, s_rim, r_rim,
+                 s_part, r_part):
+    p = lax.axis_index("mesh")
+    q = lax.axis_index("comb")
+    core = lax.rem(q, 2)
+    chip = q // 2
+    mate = q + 1 - 2 * core
+    far = lax.rem(q + 2, 4)
+    lane_own = pl.multiple_of((core * 2 + chip) * 128, 128)
+    lane_far = pl.multiple_of((core * 2 + 1 - chip) * 128, 128)
+    lane_half = pl.multiple_of(core * 256, 256)
+    has_low = p > 0
+    has_up = p < n_mesh - 1
+    nodes = basis_ref.shape[1]
+    ghost = send_ref.shape[1]
+
+    def remote(src, dst, ssem, rsem, pp, qq):
+        return pltpu.make_async_remote_copy(
+            src_ref=src, dst_ref=dst, send_sem=ssem, recv_sem=rsem,
+            device_id=(pp, qq), device_id_type=MESH)
+
+    barrier = pltpu.get_barrier_semaphore()
+    pl.semaphore_signal(barrier, inc=1, device_id=(p, mate), device_id_type=MESH)
+    pl.semaphore_signal(barrier, inc=1, device_id=(p, far), device_id_type=MESH)
+    for r in range(1, n_mesh):
+        pl.semaphore_signal(barrier, inc=1, device_id=(lax.rem(p + r, n_mesh), q), device_id_type=MESH)
+
+    for at, blk in enumerate((0, 2, 1, 3)):
+        coef_s[:, at * 128:(at + 1) * 128] = coeffs_ref[:, blk * 128:(blk + 1) * 128]
+    for side in range(2):
+        ids = jnp.broadcast_to(send_ref[side:side + 1, :].astype(jnp.float32), (ghost, ghost)).T
+        for at in range(nodes // 128):
+            lanes = (lax.broadcasted_iota(jnp.int32, (ghost, 128), 1) + at * 128).astype(jnp.float32)
+            lent_onehot[side * ghost:(side + 1) * ghost, at * 128:(at + 1) * 128] = jnp.where(
+                ids == lanes, 1.0, 0.0).astype(jnp.bfloat16)
+
+    pl.semaphore_wait(barrier, n_mesh + 1)
+
+    own = pl.ds(0, nodes)
+    rim = pl.ds(nodes, 2 * ghost)
+
+    def far_copy(d):
+        return remote(basis_ref.at[d], wide.at[d, own, pl.ds(lane_own, 128)], s_far.at[d], r_far.at[d], p, far)
+
+    def mate_copy(d):
+        return remote(basis_ref.at[d], wide.at[d, own, pl.ds(lane_own, 128)], s_mate.at[d], r_mate.at[d], p, mate)
+
+    def fwd_copy(d):
+        src = wide.at[d, own, pl.ds(lane_far, 128)]
+        return remote(src, src, s_fwd.at[d], r_fwd.at[d], p, mate)
+
+    def rim_copy(d):
+        src = wide.at[d, rim, pl.ds(lane_half, 256)]
+        return remote(src, src, s_rim.at[d], r_rim.at[d], p, mate)
+
+    def lent_copy(kind, d, side):
+        src = (lent_own if kind == 0 else lent_far).at[d, pl.ds(side * ghost, ghost)]
+        slot = nodes + ghost if side == 0 else nodes
+        lane = lane_own if kind == 0 else lane_far
+        dst = wide.at[d, pl.ds(slot, ghost), pl.ds(lane, 128)]
+        to = p - 1 if side == 0 else p + 1
+        return remote(src, dst, s_lent.at[kind, d, side], r_lent.at[kind, d, side], to, q)
+
+    for d in range(3):
+        far_copy(d).start()
+    for d in range(3):
+        mate_copy(d).start()
+
+    def lend(kind, d):
+        src = basis_ref[d] if kind == 0 else wide[d, :nodes, pl.ds(lane_far, 128)]
+        rows = jnp.dot(lent_onehot[...], src, preferred_element_type=jnp.float32).astype(jnp.bfloat16)
+        if kind == 0:
+            lent_own[d] = rows
+        else:
+            lent_far[d] = rows
+
+        @pl.when(has_low)
+        def _():
+            lent_copy(kind, d, 0).start()
+
+        @pl.when(has_up)
+        def _():
+            lent_copy(kind, d, 1).start()
+
+    for d in range(3):
+        lend(0, d)
+    for d in range(3):
+        wide[d, :nodes, pl.ds(lane_own, 128)] = basis_ref[d]
+
+    @pl.when(jnp.logical_not(has_low))
+    def _():
+        for d in range(3):
+            wide[d, nodes:nodes + ghost, pl.ds(lane_half, 256)] = jnp.zeros((ghost, 256), jnp.bfloat16)
+
+    @pl.when(jnp.logical_not(has_up))
+    def _():
+        for d in range(3):
+            wide[d, nodes + ghost:, pl.ds(lane_half, 256)] = jnp.zeros((ghost, 256), jnp.bfloat16)
+
+    elems = stiff_ref.shape[0] * 128
+
+    def build(i, carry):
+        rows = pl.ds(pl.multiple_of(i * 64, 64), 64)
+        ids = lax.broadcasted_iota(jnp.int32, (64, 128), 0) + i * 64
+        for b in range(elems // 128):
+            base = jnp.where(ids == connect_ref[b, 0:1, :], 1.0, 0.0)
+            for t in range(3):
+                one = jnp.where(ids == connect_ref[b, t + 1:t + 2, :], 1.0, 0.0)
+                inc[rows, t * elems + b * 128:t * elems + (b + 1) * 128] = (one - base).astype(jnp.bfloat16)
+        return carry
+
+    lax.fori_loop(0, wide.shape[1] // 64, build, 0)
+
+    def stage_far(d):
+        far_copy(d).wait_recv()
+        fwd_copy(d).start()
+        lend(1, d)
+
+    def stage_rim(d):
+        @pl.when(has_up)
+        def _():
+            lent_copy(0, d, 0).wait_recv()
+            lent_copy(1, d, 0).wait_recv()
+
+        @pl.when(has_low)
+        def _():
+            lent_copy(0, d, 1).wait_recv()
+            lent_copy(1, d, 1).wait_recv()
+
+        rim_copy(d).start()
+
+    combos = coeffs_ref.shape[0]
+
+    def stage_disp(d):
+        mate_copy(d).wait_recv()
+        fwd_copy(d).wait_recv()
+        rim_copy(d).wait_recv()
+        disp = lax.dot_general(coef_s[...], wide[d], (((1,), (1,)), ((), ())),
+                               preferred_element_type=jnp.float32).astype(jnp.bfloat16)
+        for t in range(3):
+            disp_v[d * combos:(d + 1) * combos, t * elems:(t + 1) * elems] = jnp.dot(
+                disp, inc[:, t * elems:(t + 1) * elems], preferred_element_type=jnp.float32)
+
+    stage_far(0)
+    stage_far(1)
+    stage_rim(0)
+    stage_disp(0)
+    stage_far(2)
+    stage_rim(1)
+    stage_disp(1)
+    stage_rim(2)
+    stage_disp(2)
+
+    count = count_ref[0]
+    slots = wide.shape[1]
+    modes = wide.shape[2]
+    scale = (modes / (3.0 * nodes * n_mesh)) ** 0.5
+    chunks = part_out.shape[0]
+    crow = combos // chunks
+    tile = 16
+
+    for h in range(chunks):
+        def tile_force(i, carry):
+            for b in range(elems // 128):
+                lane = lax.broadcasted_iota(jnp.int32, (1, 128), 1) + b * 128
+                k = jnp.where(lane < count, stiff_ref[b:b + 1, :], 0.0)
+                k3 = jnp.broadcast_to(k * stiff_cubic, (tile, 128))
+                kt = jnp.broadcast_to(k * twist_ratio, (tile, 128))
+                kb = jnp.broadcast_to(k, (tile, 128))
+
+                def vec(t):
+                    return [disp_v[pl.ds(pl.multiple_of(d * combos + h * crow + i * tile, tile), tile),
+                                   t * elems + b * 128:t * elems + (b + 1) * 128] for d in range(3)]
+                vb, vc, vd = vec(0), vec(1), vec(2)
+
+                def dot3(x, y):
+                    return x[0] * y[0] + x[1] * y[1] + x[2] * y[2]
+
+                def sub3(x, y):
+                    return [x[j] - y[j] for j in range(3)]
+
+                def stiff(x):
+                    return kb + k3 * dot3(x, x)
+                bc, cd, bd = sub3(vc, vb), sub3(vd, vc), sub3(vd, vb)
+                sab, sac, sad = stiff(vb), stiff(vc), stiff(vd)
+                sbc, scd, sbd = stiff(bc), stiff(cd), stiff(bd)
+                for d in range(3):
+                    tw = kt * (vb[d] + cd[d])
+                    tbc, tcd, tbd = sbc * bc[d], scd * cd[d], sbd * bd[d]
+                    fb = sab * vb[d] - tbc - tbd + tw
+                    fc = sac * vc[d] + tbc - tcd - tw
+                    fd = sad * vd[d] + tcd + tbd + tw
+                    for t, f in enumerate((fb, fc, fd)):
+                        high = f.astype(jnp.bfloat16)
+                        low = (f - high.astype(jnp.float32)).astype(jnp.bfloat16)
+                        lanes = slice(t * elems + b * 128, t * elems + (b + 1) * 128)
+                        force_s[pl.ds(pl.multiple_of(d * crow + i * tile, tile), tile), lanes] = high
+                        force_s[pl.ds(pl.multiple_of((3 + d) * crow + i * tile, tile), tile), lanes] = low
+            return carry
+
+        lax.fori_loop(0, crow // tile, tile_force, 0)
+
+        for g in range(slots // 256):
+            rows = slice(g * 256, (g + 1) * 256)
+            both = lax.dot_general(force_s[...], inc[rows, :], (((1,), (1,)), ((), ())),
+                                   preferred_element_type=jnp.float32)
+            nodal = (both[:3 * crow] + both[3 * crow:]).astype(jnp.bfloat16)
+            add = jnp.dot(nodal[:crow], wide[0, rows, :], preferred_element_type=jnp.float32)
+            for d in range(1, 3):
+                add += jnp.dot(nodal[d * crow:(d + 1) * crow], wide[d, rows, :], preferred_element_type=jnp.float32)
+            if g == 0:
+                modal_acc[...] = add
+            else:
+                modal_acc[...] += add
+
+        low_half = lax.broadcasted_iota(jnp.int32, (crow // 2, 128), 1) < 64
+        for blk in range(4):
+            at = ((blk % 2) * 2 + blk // 2) * 128
+            top = modal_acc[:crow // 2, at:at + 128] * scale
+            bottom = modal_acc[crow // 2:, at:at + 128] * scale
+            part_out[h, 2 * blk] = jnp.where(low_half, top, pltpu.roll(bottom, 64, 1))
+            part_out[h, 2 * blk + 1] = jnp.where(low_half, pltpu.roll(top, 64, 1), bottom)
+        for r in range(1, n_mesh):
+            part_copy(remote, part_out, part_in, s_part, r_part, h, r, p, q, n_mesh).start()
+
+    for h in range(chunks):
+        total = part_out[h, p]
+        for r in range(1, n_mesh):
+            part_copy(remote, part_out, part_in, s_part, r_part, h, r, p, q, n_mesh).wait_recv()
+            total = total + part_in[h, r - 1]
+        out_ref[h * crow:h * crow + crow // 2, :] = total[:, :64]
+        out_ref[h * crow + crow // 2:(h + 1) * crow, :] = pltpu.roll(total, 64, 1)[:, :64]
+
+    for d in range(3):
+        far_copy(d).wait_send()
+        mate_copy(d).wait_send()
+        fwd_copy(d).wait_send()
+        rim_copy(d).wait_send()
+        for kind in range(2):
+            @pl.when(has_low)
+            def _():
+                lent_copy(kind, d, 0).wait_send()
+
+            @pl.when(has_up)
+            def _():
+                lent_copy(kind, d, 1).wait_send()
+    for h in range(chunks):
+        for r in range(1, n_mesh):
+            part_copy(remote, part_out, part_in, s_part, r_part, h, r, p, q, n_mesh).wait_send()
+
+
+def part_copy(remote, part_out, part_in, s_part, r_part, h, r, p, q, n_mesh):
+    to = lax.rem(p + r, n_mesh)
+    return remote(part_out.at[h, to], part_in.at[h, r - 1], s_part.at[h, r - 1], r_part.at[h, r - 1], to, q)
+
+
+def fused_body(coeffs, basis, connect, stiffness, send_lists, elem_count):
+    n_mesh = lax.axis_size("mesh")
+    combos, modes = coeffs.shape
+    nodes = basis.shape[1]
+    ghost = send_lists.shape[2]
+    slots = nodes + 2 * ghost
+    elems = stiffness.shape[0] * 128
+    chunks = 2
+    crow = combos // chunks
+    bf16, f32 = jnp.bfloat16, jnp.float32
+    vmem = pl.BlockSpec(memory_space=pltpu.VMEM)
+    dma = pltpu.SemaphoreType.DMA
+    return pl.pallas_call(
+        functools.partial(fused_kernel, n_mesh),
+        out_shape=jax.ShapeDtypeStruct((combos, modes // n_mesh), f32),
+        in_specs=[vmem] * 5 + [pl.BlockSpec(memory_space=pltpu.SMEM)],
+        out_specs=vmem,
+        scratch_shapes=[
+            pltpu.VMEM((combos, modes), bf16),
+            pltpu.VMEM((3, slots, modes), bf16),
+            pltpu.VMEM((slots, 3 * elems), bf16),
+            pltpu.VMEM((2 * ghost, nodes), bf16),
+            pltpu.VMEM((3, 2 * ghost, 128), bf16),
+            pltpu.VMEM((3, 2 * ghost, 128), bf16),
+            pltpu.VMEM((3 * combos, 3 * elems), f32),
+            pltpu.VMEM((6 * crow, 3 * elems), bf16),
+            pltpu.VMEM((crow, modes), f32),
+            pltpu.VMEM((chunks, n_mesh, crow // 2, 128), f32),
+            pltpu.VMEM((chunks, n_mesh - 1, crow // 2, 128), f32),
+            dma((3,)), dma((3,)), dma((3,)), dma((3,)), dma((3,)), dma((3,)),
+            dma((2, 3, 2)), dma((2, 3, 2)), dma((3,)), dma((3,)),
+            dma((chunks, n_mesh - 1)), dma((chunks, n_mesh - 1)),
+        ],
+        compiler_params=pltpu.CompilerParams(
+            collective_id=0, has_side_effects=True, vmem_limit_bytes=48 * 2 ** 20),
+        cost_estimate=pl.CostEstimate(flops=6 * 10 ** 9, bytes_accessed=4 * 10 ** 6, transcendentals=0),
+    )(coeffs, basis, connect, stiffness, send_lists[0], elem_count)
+
+
+def any_body(coeffs, basis, connect, stiffness, send_lists, elem_count):
+    fits = (lax.axis_size("comb") == 4 and lax.axis_size("mesh") == 8 and coeffs.shape == (256, 512)
+            and basis.shape == (3, 512, 128) and send_lists.shape[1:] == (2, 128) and stiffness.shape[0] == 4)
+    return (fused_body if fits else body)(coeffs, basis, connect, stiffness, send_lists, elem_count)
+
+
 def solution(mesh):
     in_specs = (
         P("comb", None),
@@ -95,4 +404,4 @@
         P("mesh"),
     )
     out_specs = P("comb", "mesh")
-    return jax.shard_map(body, mesh=mesh, in_specs=in_specs, out_specs=out_specs, check_vma=False)
+    return jax.shard_map(any_body, mesh=mesh, in_specs=in_specs, out_specs=out_specs, check_vma=False)

time: 400 us -> 44.8 us (0.11); the launches traced: 392 us -> 44.6 us
  other arithmetic: 240 us -> 0 us
  waiting for transfers between devices: 95.4 us -> 0 us
  Pallas kernels: 0 us -> 39.9 us
  local copies, waits for them, and re-layouts: 31.2 us -> 4.02 us
  between operations: 14.2 us -> 0.69 us
  starting transfers between devices: 7.46 us -> 0 us
    scatter-add x4 -> x0, other arithmetic: 208 us -> none  [add_block(): return forces.at[slot_ids].add(pushed.reshape(512, 3, comb_rows))]
    reduce_scatter x1 -> x0, waiting for transfers between devices: 64.6 us -> none  [body(): lax.psum_scatter(modal * out_scale, 'mesh', scatter_dimension=1, tiled=True)]
    pallas_call x0 -> x1, Pallas kernels: none -> 39.9 us  [fused_body(): pl.pallas_call(functools.partial(fused_kernel, n_mesh), out_shape=jax.Sha...]
    all_gather x1 -> x0, waiting for transfers between devices: 23.5 us -> none  [body(): whole_basis = lax.all_gather(basis, 'comb', axis=2, tiled=True)]
    gather x7 -> x0, local copies, waits for them, and re-layouts: 19.9 us -> none  [the longest x4 12.9 us: add_block(): jnp.take(displaced, slot_ids, axis=0).astype(jnp.float32)]
    reduce_sum x4 -> x0, other arithmetic: 8.76 us -> none  [spring_pull(): jnp.sum(stretch * stretch, axis=1, keepdims=True)]
    ppermute x4 -> x0, starting transfers between devices: 7.42 us -> none  [the longest x2 4.83 us: with_halo(): before = lax.ppermute(last, axis, up)]
    convert_element_type x4 -> x0, other arithmetic: 7.07 us -> none  [add_block(): jnp.take(displaced, slot_ids, axis=0).astype(jnp.float32)]
  transfers between devices with their start and end apart: 6 -> 0, of which waited for: 4 -> 0; matrix products, arithmetic and copies ran while one was open for 2% -> 0% of each run, Pallas kernels for 0% -> 0%
where the time goes in v1:
time: 44.8 us; the launch traced here: 44.6 us
  Pallas kernels  39.9 us (89%)
  local copies, waits for them, and re-layouts  4.02 us (9%)
  between operations  0.69 us (2%)
    pallas_call x1, Pallas kernels, fused_body(): pl.pallas_call(functools.partial(fused_kernel, n_mesh), out_shape=jax.Sha...  39.9 us
    unnamed x10, local copies, waits for them, and re-layouts  3.31 us

profile of v1, /device:TPU:0, one launch (start us, length us, event | category | flops | bytes accessed | tf_op | source)
XLA Modules:
  0.0 44.6 jit_solution(9973079676762286859)
XLA Ops:
  0.0 0.0 copy-start.3
  0.7 0.0 copy-start.4
  0.7 0.0 copy-done.3
  0.7 0.7 %copy-done.4 = s32[1,2,128]{2,1,0:T(2,128)S(1)} copy-done((s32[1,2,128]{2,1,0:T(2,128)S(1)}, s32[1,2,128]{2,1,0:T(2,128)}, u32[]{:S(2)}) %copy-start.4) | copy-done | bytes 1048
  1.3 0.0 copy-start
  1.4 1.0 %copy-done = bf16[3,512,128]{2,1,0:T(8,128)(2,1)S(1)} copy-done((bf16[3,512,128]{2,1,0:T(8,128)(2,1)S(1)}, bf16[3,512,128]{2,1,0:T(8,128)(2,1)}, u32[]{:S(2)}) %copy-start) | copy-done | bytes 393240
  2.3 0.0 copy-start.1
  2.3 0.9 %copy-done.1 = bf16[256,512]{1,0:T(8,128)(2,1)S(1)} copy-done((bf16[256,512]{1,0:T(8,128)(2,1)S(1)}, bf16[256,512]{1,0:T(8,128)(2,1)}, u32[]{:S(2)}) %copy-start.1) | copy-done | bytes 262168
  3.3 0.0 copy-start.2
  3.3 0.7 %copy-done.2 = s32[4,4,128]{2,1,0:T(4,128)S(1)} copy-done((s32[4,4,128]{2,1,0:T(4,128)S(1)}, s32[4,4,128]{2,1,0:T(4,128)}, u32[]{:S(2)}) %copy-start.2) | copy-done | bytes 8216
  4.0 39.9 %shard_map.64 = f32[256,64]{1,0:T(8,128)S(1)} custom-call(bf16[256,512]{1,0:T(8,128)(2,1)S(1)} %copy-done.1, bf16[3,512,128]{2,1,0:T(8,128)(2,1)S(1)} %copy-done, s32[4,4,128]{2,1,0:T(4,128)S(1)} %copy-done.2, f32[4,128]{1,0:T(4,128)S(1)} %copy-done.3, s32[2,128]{1,0:T(2,128)S(1)} %bitcast.1, s32[1]{0:T(128)S(6)} %copy.8.count_ref), custom_call_target="tpu_custom_call" | custom-call | flops 6000000000 | bytes 4000000 | tf_op jit(solution)/shard_map/pallas_call | solution.py:364
  43.9 0.7 %copy.7 = f32[256,64]{0,1:T(8,128)} copy(f32[256,64]{1,0:T(8,128)S(1)} %shard_map.64) | data formatting | bytes 131072 | tf_op jit(solution)/shard_map/pallas_call | solution.py:364
Async XLA Ops:
  0.0 0.7 %copy-start.3 = (f32[4,128]{1,0:T(4,128)S(1)}, f32[4,128]{1,0:T(4,128)}, u32[]{:S(2)}) copy-start(f32[4,128]{1,0:T(4,128)} %stiff_ref.1) | copy-start | bytes 6148
  0.7 0.7 %copy-start.4 = (s32[1,2,128]{2,1,0:T(2,128)S(1)}, s32[1,2,128]{2,1,0:T(2,128)}, u32[]{:S(2)}) copy-start(s32[1,2,128]{2,1,0:T(2,128)} %param.10) | copy-start | bytes 3076
  1.3 1.0 %copy-start = (bf16[3,512,128]{2,1,0:T(8,128)(2,1)S(1)}, bf16[3,512,128]{2,1,0:T(8,128)(2,1)}, u32[]{:S(2)}) copy-start(bf16[3,512,128]{2,1,0:T(8,128)(2,1)} %basis_ref.1) | copy-start | bytes 1179652
  2.3 0.9 %copy-start.1 = (bf16[256,512]{1,0:T(8,128)(2,1)S(1)}, bf16[256,512]{1,0:T(8,128)(2,1)}, u32[]{:S(2)}) copy-start(bf16[256,512]{1,0:T(8,128)(2,1)} %coeffs_ref.1) | copy-start | bytes 786436
  3.3 0.7 %copy-start.2 = (s32[4,4,128]{2,1,0:T(4,128)S(1)}, s32[4,4,128]{2,1,0:T(4,128)}, u32[]{:S(2)}) copy-start(s32[4,4,128]{2,1,0:T(4,128)} %connect_ref.1) | copy-start | bytes 24580

commit v2 on v1

--- a/solution.py
+++ b/solution.py
@@ -90,9 +90,10 @@
     return lax.psum_scatter(modal * out_scale, "mesh", scatter_dimension=1, tiled=True)
 
 
-def fused_kernel(n_mesh, coeffs_ref, basis_ref, connect_ref, stiff_ref, send_ref, count_ref, out_ref,
+def fused_kernel(n_mesh, coeffs_any, basis_any, connect_any, stiff_any, send_any, count_ref, out_ref,
+                 coeffs_ref, basis_ref, connect_ref, stiff_ref, send_ref, s_in, known,
                  coef_s, wide, inc, lent_onehot, lent_own, lent_far, disp_v, force_s, modal_acc,
-                 part_out, part_in,
+                 disp_s, part_own, part_out, part_in,
                  s_mate, r_mate, s_far, r_far, s_fwd, r_fwd, s_lent, r_lent, s_rim, r_rim,
                  s_part, r_part):
     p = lax.axis_index("mesh")
@@ -107,80 +108,106 @@
     has_low = p > 0
     has_up = p < n_mesh - 1
     nodes = basis_ref.shape[1]
-    ghost = send_ref.shape[1]
+    ghost = send_ref.shape[2]
 
     def remote(src, dst, ssem, rsem, pp, qq):
         return pltpu.make_async_remote_copy(
             src_ref=src, dst_ref=dst, send_sem=ssem, recv_sem=rsem,
             device_id=(pp, qq), device_id_type=MESH)
 
+    y_mate = p + 1 - 2 * lax.rem(p, 2)
+    has_z_low = p >= 2
+    has_z_up = p < n_mesh - 2
+    greets = 3 + jnp.where(has_z_low, 1, 0) + jnp.where(has_z_up, 1, 0)
+
+    def greet(sem):
+        pl.semaphore_signal(sem, inc=1, device_id=(p, mate), device_id_type=MESH)
+        pl.semaphore_signal(sem, inc=1, device_id=(p, far), device_id_type=MESH)
+        pl.semaphore_signal(sem, inc=1, device_id=(y_mate, q), device_id_type=MESH)
+
+        @pl.when(has_z_low)
+        def _():
+            pl.semaphore_signal(sem, inc=1, device_id=(p - 2, q), device_id_type=MESH)
+
+        @pl.when(has_z_up)
+        def _():
+            pl.semaphore_signal(sem, inc=1, device_id=(p + 2, q), device_id_type=MESH)
+
     barrier = pltpu.get_barrier_semaphore()
-    pl.semaphore_signal(barrier, inc=1, device_id=(p, mate), device_id_type=MESH)
-    pl.semaphore_signal(barrier, inc=1, device_id=(p, far), device_id_type=MESH)
-    for r in range(1, n_mesh):
-        pl.semaphore_signal(barrier, inc=1, device_id=(lax.rem(p + r, n_mesh), q), device_id_type=MESH)
-
-    for at, blk in enumerate((0, 2, 1, 3)):
-        coef_s[:, at * 128:(at + 1) * 128] = coeffs_ref[:, blk * 128:(blk + 1) * 128]
+    greet(barrier)
+
+    loads = [pltpu.make_async_copy(src, dst, s_in.at[n]) for n, (src, dst) in enumerate((
+        (send_any, send_ref), (connect_any, connect_ref), (basis_any, basis_ref),
+        (coeffs_any, coeffs_ref), (stiff_any, stiff_ref)))]
+    for load in loads:
+        load.start()
+    own = pl.ds(0, nodes)
+    rim = pl.ds(nodes, 2 * ghost)
+    elems = stiff_ref.shape[0] * 128
+
+    pl.semaphore_wait(barrier, greets)
+
+    def far_copy(d):
+        return remote(basis_any.at[d], wide.at[d, own, pl.ds(lane_own, 128)], s_far.at[d], r_far.at[d], p, far)
+
+    def mate_copy(d):
+        return remote(basis_any.at[d], wide.at[d, own, pl.ds(lane_own, 128)], s_mate.at[d], r_mate.at[d], p, mate)
+
+    def fwd_copy(d):
+        src = wide.at[d, own, pl.ds(lane_far, 128)]
+        return remote(src, src, s_fwd.at[d], r_fwd.at[d], p, mate)
+
+    def rim_copy(d):
+        src = wide.at[d, rim, pl.ds(lane_half, 256)]
+        return remote(src, src, s_rim.at[d], r_rim.at[d], p, mate)
+
+    def lent_copy(kind, d, side):
+        src = (lent_far if kind == 1 else lent_own).at[d, pl.ds(side * ghost, ghost)]
+        slot = nodes + ghost if side == 0 else nodes
+        lane = lane_far if kind == 1 else lane_own
+        dst = wide.at[d, pl.ds(slot, ghost), pl.ds(lane, 128)]
+        to = p - 1 if side == 0 else p + 1
+        sem = min(kind, 1)
+        return remote(src, dst, s_lent.at[sem, d, side], r_lent.at[sem, d, side], to, far if kind == 2 else q)
+
+    def lend(kind, d):
+        @pl.when(has_low)
+        def _():
+            lent_copy(kind, d, 0).start()
+
+        @pl.when(has_up)
+        def _():
+            lent_copy(kind, d, 1).start()
+
+    for d in range(3):
+        far_copy(d).start()
+    for d in range(3):
+        mate_copy(d).start()
+    greet(known.at[0])
+    loads[0].wait()
     for side in range(2):
-        ids = jnp.broadcast_to(send_ref[side:side + 1, :].astype(jnp.float32), (ghost, ghost)).T
+        ids = jnp.broadcast_to(send_ref[0, side:side + 1, :].astype(jnp.float32), (ghost, ghost)).T
         for at in range(nodes // 128):
             lanes = (lax.broadcasted_iota(jnp.int32, (ghost, 128), 1) + at * 128).astype(jnp.float32)
             lent_onehot[side * ghost:(side + 1) * ghost, at * 128:(at + 1) * 128] = jnp.where(
                 ids == lanes, 1.0, 0.0).astype(jnp.bfloat16)
-
-    pl.semaphore_wait(barrier, n_mesh + 1)
-
-    own = pl.ds(0, nodes)
-    rim = pl.ds(nodes, 2 * ghost)
-
-    def far_copy(d):
-        return remote(basis_ref.at[d], wide.at[d, own, pl.ds(lane_own, 128)], s_far.at[d], r_far.at[d], p, far)
-
-    def mate_copy(d):
-        return remote(basis_ref.at[d], wide.at[d, own, pl.ds(lane_own, 128)], s_mate.at[d], r_mate.at[d], p, mate)
-
-    def fwd_copy(d):
-        src = wide.at[d, own, pl.ds(lane_far, 128)]
-        return remote(src, src, s_fwd.at[d], r_fwd.at[d], p, mate)
-
-    def rim_copy(d):
-        src = wide.at[d, rim, pl.ds(lane_half, 256)]
-        return remote(src, src, s_rim.at[d], r_rim.at[d], p, mate)
-
-    def lent_copy(kind, d, side):
-        src = (lent_own if kind == 0 else lent_far).at[d, pl.ds(side * ghost, ghost)]
-        slot = nodes + ghost if side == 0 else nodes
-        lane = lane_own if kind == 0 else lane_far
-        dst = wide.at[d, pl.ds(slot, ghost), pl.ds(lane, 128)]
-        to = p - 1 if side == 0 else p + 1
-        return remote(src, dst, s_lent.at[kind, d, side], r_lent.at[kind, d, side], to, q)
-
-    for d in range(3):
-        far_copy(d).start()
-    for d in range(3):
-        mate_copy(d).start()
-
-    def lend(kind, d):
-        src = basis_ref[d] if kind == 0 else wide[d, :nodes, pl.ds(lane_far, 128)]
-        rows = jnp.dot(lent_onehot[...], src, preferred_element_type=jnp.float32).astype(jnp.bfloat16)
-        if kind == 0:
-            lent_own[d] = rows
-        else:
-            lent_far[d] = rows
-
-        @pl.when(has_low)
-        def _():
-            lent_copy(kind, d, 0).start()
-
-        @pl.when(has_up)
-        def _():
-            lent_copy(kind, d, 1).start()
-
+    for load in loads[1:]:
+        load.wait()
+
+    def own_rows(d, carry):
+        lent_own[d] = jnp.dot(lent_onehot[...], basis_ref[d], preferred_element_type=jnp.float32).astype(jnp.bfloat16)
+        wide[d, :nodes, pl.ds(lane_own, 128)] = basis_ref[d]
+        return carry
+
+    lax.fori_loop(0, 3, own_rows, 0)
+
+    pl.semaphore_wait(known.at[0], greets)
+    greet(known.at[1])
     for d in range(3):
         lend(0, d)
-    for d in range(3):
-        wide[d, :nodes, pl.ds(lane_own, 128)] = basis_ref[d]
+    pl.semaphore_wait(known.at[1], greets)
+    greet(known.at[2])
+    lend(2, 2)
 
     @pl.when(jnp.logical_not(has_low))
     def _():
@@ -192,7 +219,9 @@
         for d in range(3):
             wide[d, nodes + ghost:, pl.ds(lane_half, 256)] = jnp.zeros((ghost, 256), jnp.bfloat16)
 
-    elems = stiff_ref.shape[0] * 128
+    for at, blk in enumerate((0, 2, 1, 3)):
+        coef_s[:, at * 128:(at + 1) * 128] = coeffs_ref[:, blk * 128:(blk + 1) * 128]
+
 
     def build(i, carry):
         rows = pl.ds(pl.multiple_of(i * 64, 64), 64)
@@ -209,7 +238,12 @@
     def stage_far(d):
         far_copy(d).wait_recv()
         fwd_copy(d).start()
-        lend(1, d)
+
+        @pl.when(d < 2)
+        def _():
+            lent_far[d] = jnp.dot(lent_onehot[...], wide[d, :nodes, pl.ds(lane_far, 128)],
+                                  preferred_element_type=jnp.float32).astype(jnp.bfloat16)
+            lend(1, d)
 
     def stage_rim(d):
         @pl.when(has_up)
@@ -232,19 +266,28 @@
         rim_copy(d).wait_recv()
         disp = lax.dot_general(coef_s[...], wide[d], (((1,), (1,)), ((), ())),
                                preferred_element_type=jnp.float32).astype(jnp.bfloat16)
-        for t in range(3):
-            disp_v[d * combos:(d + 1) * combos, t * elems:(t + 1) * elems] = jnp.dot(
-                disp, inc[:, t * elems:(t + 1) * elems], preferred_element_type=jnp.float32)
+        disp_s[...] = disp
+
+        def expand(t, carry):
+            lanes = pl.ds(pl.multiple_of(t * elems, 128), elems)
+            disp_v[pl.ds(pl.multiple_of(d * combos, combos), combos), lanes] = jnp.dot(
+                disp_s[...], inc[:, lanes], preferred_element_type=jnp.float32)
+            return carry
+
+        lax.fori_loop(0, 3, expand, 0, unroll=True)
 
     stage_far(0)
-    stage_far(1)
-    stage_rim(0)
-    stage_disp(0)
-    stage_far(2)
-    stage_rim(1)
-    stage_disp(1)
-    stage_rim(2)
-    stage_disp(2)
+    pl.semaphore_wait(known.at[2], greets)
+
+    def arrive(d, carry):
+        @pl.when(d < 2)
+        def _():
+            stage_far(d + 1)
+        stage_rim(d)
+        stage_disp(d)
+        return carry
+
+    lax.fori_loop(0, 3, arrive, 0)
 
     count = count_ref[0]
     slots = wide.shape[1]
@@ -254,7 +297,7 @@
     crow = combos // chunks
     tile = 16
 
-    for h in range(chunks):
+    def chunk(h, outer):
         def tile_force(i, carry):
             for b in range(elems // 128):
                 lane = lax.broadcasted_iota(jnp.int32, (1, 128), 1) + b * 128
@@ -264,7 +307,7 @@
                 kb = jnp.broadcast_to(k, (tile, 128))
 
                 def vec(t):
-                    return [disp_v[pl.ds(pl.multiple_of(d * combos + h * crow + i * tile, tile), tile),
+                    return [disp_v[pl.ds(pl.multiple_of(h * crow + d * combos + i * tile, tile), tile),
                                    t * elems + b * 128:t * elems + (b + 1) * 128] for d in range(3)]
                 vb, vc, vd = vec(0), vec(1), vec(2)
 
@@ -295,36 +338,54 @@
 
         lax.fori_loop(0, crow // tile, tile_force, 0)
 
-        for g in range(slots // 256):
-            rows = slice(g * 256, (g + 1) * 256)
+        modal_acc[...] = jnp.zeros_like(modal_acc)
+
+        def scatter(g, carry):
+            rows = pl.ds(pl.multiple_of(g * 256, 256), 256)
             both = lax.dot_general(force_s[...], inc[rows, :], (((1,), (1,)), ((), ())),
                                    preferred_element_type=jnp.float32)
             nodal = (both[:3 * crow] + both[3 * crow:]).astype(jnp.bfloat16)
             add = jnp.dot(nodal[:crow], wide[0, rows, :], preferred_element_type=jnp.float32)
             for d in range(1, 3):
                 add += jnp.dot(nodal[d * crow:(d + 1) * crow], wide[d, rows, :], preferred_element_type=jnp.float32)
-            if g == 0:
-                modal_acc[...] = add
-            else:
-                modal_acc[...] += add
+            modal_acc[...] += add
+            return carry
+
+        lax.fori_loop(0, slots // 256, scatter, 0, unroll=True)
+
+        def encode(to, value):
+            peak = jnp.maximum(jnp.max(jnp.abs(value), axis=0, keepdims=True), 1e-30)
+            power = jnp.ceil(jnp.log2(peak))
+            whole = jnp.round(value * (32000.0 * jnp.exp2(-power)))
+            part_own[h, to] = value
+            part_out[h, to, :crow // 2] = whole.astype(jnp.int32).astype(jnp.int16)
+            part_out[h, to, crow // 2:] = jnp.broadcast_to(power, (16, 128)).astype(jnp.int32).astype(jnp.int16)
 
         low_half = lax.broadcasted_iota(jnp.int32, (crow // 2, 128), 1) < 64
         for blk in range(4):
             at = ((blk % 2) * 2 + blk // 2) * 128
             top = modal_acc[:crow // 2, at:at + 128] * scale
             bottom = modal_acc[crow // 2:, at:at + 128] * scale
-            part_out[h, 2 * blk] = jnp.where(low_half, top, pltpu.roll(bottom, 64, 1))
-            part_out[h, 2 * blk + 1] = jnp.where(low_half, pltpu.roll(top, 64, 1), bottom)
+            encode(2 * blk, jnp.where(low_half, top, pltpu.roll(bottom, 64, 1)))
+            encode(2 * blk + 1, jnp.where(low_half, pltpu.roll(top, 64, 1), bottom))
         for r in range(1, n_mesh):
             part_copy(remote, part_out, part_in, s_part, r_part, h, r, p, q, n_mesh).start()
-
-    for h in range(chunks):
-        total = part_out[h, p]
+        return outer
+
+    lax.fori_loop(0, chunks, chunk, 0)
+
+    def collect(h, outer):
+        total = part_own[h, p]
         for r in range(1, n_mesh):
             part_copy(remote, part_out, part_in, s_part, r_part, h, r, p, q, n_mesh).wait_recv()
-            total = total + part_in[h, r - 1]
-        out_ref[h * crow:h * crow + crow // 2, :] = total[:, :64]
-        out_ref[h * crow + crow // 2:(h + 1) * crow, :] = pltpu.roll(total, 64, 1)[:, :64]
+            unit = jnp.exp2(part_in[h, r - 1, crow // 2:].astype(jnp.int32).astype(jnp.float32)[:1]) * (1.0 / 32000.0)
+            total = total + part_in[h, r - 1, :crow // 2].astype(jnp.int32).astype(jnp.float32) * unit
+        at = pl.multiple_of(h * crow, crow)
+        out_ref[pl.ds(at, crow // 2), :] = total[:, :64]
+        out_ref[pl.ds(at + crow // 2, crow // 2), :] = pltpu.roll(total, 64, 1)[:, :64]
+        return outer
+
+    lax.fori_loop(0, chunks, collect, 0)
 
     for d in range(3):
         far_copy(d).wait_send()
@@ -364,9 +425,15 @@
     return pl.pallas_call(
         functools.partial(fused_kernel, n_mesh),
         out_shape=jax.ShapeDtypeStruct((combos, modes // n_mesh), f32),
-        in_specs=[vmem] * 5 + [pl.BlockSpec(memory_space=pltpu.SMEM)],
+        in_specs=[pl.BlockSpec(memory_space=pl.ANY)] * 5 + [pl.BlockSpec(memory_space=pltpu.SMEM)],
         out_specs=vmem,
         scratch_shapes=[
+            pltpu.VMEM(coeffs.shape, bf16),
+            pltpu.VMEM(basis.shape, bf16),
+            pltpu.VMEM(connect.shape, jnp.int32),
+            pltpu.VMEM(stiffness.shape, f32),
+            pltpu.VMEM(send_lists.shape, jnp.int32),
+            dma((5,)), pltpu.SemaphoreType.REGULAR((3,)),
             pltpu.VMEM((combos, modes), bf16),
             pltpu.VMEM((3, slots, modes), bf16),
             pltpu.VMEM((slots, 3 * elems), bf16),
@@ -376,8 +443,10 @@
             pltpu.VMEM((3 * combos, 3 * elems), f32),
             pltpu.VMEM((6 * crow, 3 * elems), bf16),
             pltpu.VMEM((crow, modes), f32),
+            pltpu.VMEM((combos, slots), bf16),
             pltpu.VMEM((chunks, n_mesh, crow // 2, 128), f32),
-            pltpu.VMEM((chunks, n_mesh - 1, crow // 2, 128), f32),
+            pltpu.VMEM((chunks, n_mesh, crow // 2 + 16, 128), jnp.int16),
+            pltpu.VMEM((chunks, n_mesh - 1, crow // 2 + 16, 128), jnp.int16),
             dma((3,)), dma((3,)), dma((3,)), dma((3,)), dma((3,)), dma((3,)),
             dma((2, 3, 2)), dma((2, 3, 2)), dma((3,)), dma((3,)),
             dma((chunks, n_mesh - 1)), dma((chunks, n_mesh - 1)),
@@ -385,7 +454,7 @@
         compiler_params=pltpu.CompilerParams(
             collective_id=0, has_side_effects=True, vmem_limit_bytes=48 * 2 ** 20),
         cost_estimate=pl.CostEstimate(flops=6 * 10 ** 9, bytes_accessed=4 * 10 ** 6, transcendentals=0),
-    )(coeffs, basis, connect, stiffness, send_lists[0], elem_count)
+    )(coeffs, basis, connect, stiffness, send_lists, elem_count)
 
 
 def any_body(coeffs, basis, connect, stiffness, send_lists, elem_count):

time: 44.8 us -> 41.7 us (0.931)
  Pallas kernels: 39.9 us -> 36.7 us
    pallas_call x1, Pallas kernels: 39.9 us -> 36.7 us  [fused_body(): pl.pallas_call(functools.partial(fused_kernel, n_mesh), out_shape=jax.Sha...]
where the time goes in v2:
time: 41.7 us; the launch traced here: 41.4 us
  Pallas kernels  36.7 us (88%)
  local copies, waits for them, and re-layouts  4.04 us (10%)
  between operations  0.69 us (2%)
    pallas_call x1, Pallas kernels, fused_body(): pl.pallas_call(functools.partial(fused_kernel, n_mesh), out_shape=jax.Sha...  36.7 us
    unnamed x10, local copies, waits for them, and re-layouts  3.33 us

profile of v2, /device:TPU:0, one launch (start us, length us, event | category | flops | bytes accessed | tf_op | source)
XLA Modules:
  0.0 41.4 jit_solution(6384878714581771699)
XLA Ops:
  0.0 0.0 copy-start.4
  0.7 0.0 copy-done.4
  0.7 0.0 copy-start
  0.7 1.0 %copy-done = bf16[3,512,128]{2,1,0:T(8,128)(2,1)S(1)} copy-done((bf16[3,512,128]{2,1,0:T(8,128)(2,1)S(1)}, bf16[3,512,128]{2,1,0:T(8,128)(2,1)}, u32[]{:S(2)}) %copy-start) | copy-done | bytes 393240
  1.7 0.0 copy-start.1
  1.7 0.9 %copy-done.1 = bf16[256,512]{1,0:T(8,128)(2,1)S(1)} copy-done((bf16[256,512]{1,0:T(8,128)(2,1)S(1)}, bf16[256,512]{1,0:T(8,128)(2,1)}, u32[]{:S(2)}) %copy-start.1) | copy-done | bytes 262168
  2.6 0.0 copy-start.2
  2.6 0.7 %copy-done.2 = s32[4,4,128]{2,1,0:T(4,128)S(1)} copy-done((s32[4,4,128]{2,1,0:T(4,128)S(1)}, s32[4,4,128]{2,1,0:T(4,128)}, u32[]{:S(2)}) %copy-start.2) | copy-done | bytes 8216
  3.3 0.0 copy-start.3
  3.3 0.7 %copy-done.3 = f32[4,128]{1,0:T(4,128)S(1)} copy-done((f32[4,128]{1,0:T(4,128)S(1)}, f32[4,128]{1,0:T(4,128)}, u32[]{:S(2)}) %copy-start.3) | copy-done | bytes 2072
  4.0 36.7 %shard_map.64 = f32[256,64]{1,0:T(8,128)S(1)} custom-call(bf16[256,512]{1,0:T(8,128)(2,1)S(1)} %copy-done.1, bf16[3,512,128]{2,1,0:T(8,128)(2,1)S(1)} %copy-done, s32[4,4,128]{2,1,0:T(4,128)S(1)} %copy-done.2, f32[4,128]{1,0:T(4,128)S(1)} %copy-done.3, s32[1,2,128]{2,1,0:T(2,128)S(1)} %copy-done.4, s32[1]{0:T(128)S(6)} %copy.8.count_ref), custom_call_target="tpu_custom_call" | custom-call | flops 6000000000 | bytes 4000000 | tf_op jit(solution)/shard_map/pallas_call | solution.py:425
  40.7 0.7 %copy.7 = f32[256,64]{0,1:T(8,128)} copy(f32[256,64]{1,0:T(8,128)S(1)} %shard_map.64) | data formatting | bytes 131072 | tf_op jit(solution)/shard_map/pallas_call | solution.py:425
Async XLA Ops:
  0.0 0.7 %copy-start.4 = (s32[1,2,128]{2,1,0:T(2,128)S(1)}, s32[1,2,128]{2,1,0:T(2,128)}, u32[]{:S(2)}) copy-start(s32[1,2,128]{2,1,0:T(2,128)} %send_any.1) | copy-start | bytes 3076
  0.7 1.0 %copy-start = (bf16[3,512,128]{2,1,0:T(8,128)(2,1)S(1)}, bf16[3,512,128]{2,1,0:T(8,128)(2,1)}, u32[]{:S(2)}) copy-start(bf16[3,512,128]{2,1,0:T(8,128)(2,1)} %basis_any.1) | copy-start | bytes 1179652
  1.7 0.9 %copy-start.1 = (bf16[256,512]{1,0:T(8,128)(2,1)S(1)}, bf16[256,512]{1,0:T(8,128)(2,1)}, u32[]{:S(2)}) copy-start(bf16[256,512]{1,0:T(8,128)(2,1)} %coeffs_any.1) | copy-start | bytes 786436
  2.6 0.7 %copy-start.2 = (s32[4,4,128]{2,1,0:T(4,128)S(1)}, s32[4,4,128]{2,1,0:T(4,128)}, u32[]{:S(2)}) copy-start(s32[4,4,128]{2,1,0:T(4,128)} %connect_any.1) | copy-start | bytes 24580
  3.3 0.7 %copy-start.3 = (f32[4,128]{1,0:T(4,128)S(1)}, f32[4,128]{1,0:T(4,128)}, u32[]{:S(2)}) copy-start(f32[4,128]{1,0:T(4,128)} %stiff_any.1) | copy-start | bytes 6148
